TPU v7x, 32 devices: a whole 2x2x4 slice. The times are simulated.
32 devices in a mesh: groups: 2 (over x), ctx: 8 (over z, y), dp: 2 (over core).
Axes of the slice: x: 2, y: 2, z: 4, core: 2. Of those that a mesh axis runs over, the one named last changes fastest.
Arguments:
- activations: bfloat16 [2, 8, 2560, 4096], P(None, ('groups', 'dp'), 'ctx'), parts along dimension 1, may hold values from -6 to 6
- out_grads: bfloat16 [2, 8, 2560, 4096], P(None, ('groups', 'dp'), 'ctx'), parts along dimension 1, may hold values from -6 to 6
- input_basis: bfloat16 [2, 4096, 64], replicated, may hold values from -0.09375 to 0.09375
- output_basis: bfloat16 [2, 4096, 64], replicated, may hold values from -0.09375 to 0.09375
- query_grads: float32 [256, 8192], P(('groups', 'ctx', 'dp')), parts along dimension 0, may hold values from -0.0625 to 0.0625
- doc_length: int32 [8], P(('groups', 'dp')), parts along dimension 0, may hold values from 640 to 2560, as said below
- doc_rank: int32 [8], P('groups'), parts along dimension 0, may hold values from 0 to 3, each once
Outputs:
- scores: float32 [8, 128], P(('groups', 'dp')), parts along dimension 0
There are 2 independent parts, one for each index of `groups`. A program takes and returns all parts, laid end to end along the dimension named above; an argument that names none is the same for every part. Nothing has to cross between parts.
Inputs may be any that keep to these rules, and one draw needn't show every extreme that they name: `doc_length`: some document has all 2560 tokens valid in every draw. `doc_rank`: each row number once.
All inputs are finite; a program needn't handle non-finite values.
Results may differ from a plain program's by a relative error of at most 0.0043.
Values sent between devices are 32-bit elements; how exact they have to be, the bound alone decides.
No kernel may reach another device: no remote copies, remote signals or barrier semaphores. Data moves between devices by JAX's collectives and lax.ppermute only.
A program may use at most 128 MiB of HBM per device.

v0:
```python
import functools

import jax
import jax.numpy as jnp
from jax import lax
from jax.experimental import pallas as pl
from jax.experimental.pallas import tpu as pltpu
from jax.sharding import PartitionSpec as P

LANES = 128
BY_LAST = (((1,), (1,)), ((), ()))
BY_FIRST = (((0,), (0,)), ((), ()))


def partial_kernel(
    length_ref, act_ref, outg_ref, inb_ref, outb_ref, query_ref, send_ref,
    act_buf, outg_buf, inb, outb, square, act_sem, outg_sem, basis_sem,
):
    layers, docs, tok, _ = act_ref.shape
    rank = inb_ref.shape[1]
    peers = send_ref.shape[0]
    per_layer = peers // layers
    rows = rank * rank // LANES // per_layer
    many = query_ref.shape[0]
    first = lax.axis_index("ctx") * tok
    pairs = [(layer, doc) for layer in range(layers) for doc in range(docs)]

    def copies(i):
        layer, doc = pairs[i]
        return (
            pltpu.make_async_copy(outg_ref.at[layer, doc], outg_buf.at[i], outg_sem.at[i]),
            pltpu.make_async_copy(act_ref.at[layer, doc], act_buf.at[i], act_sem.at[i]),
        )

    def bases(layer):
        return (
            pltpu.make_async_copy(outb_ref.at[layer], outb.at[layer], basis_sem.at[layer, 0]),
            pltpu.make_async_copy(inb_ref.at[layer], inb.at[layer], basis_sem.at[layer, 1]),
        )

    def has_tokens(doc):
        return first < length_ref[doc]

    for i, (layer, doc) in enumerate(pairs):
        if doc == 0:
            for copy in bases(layer):
                copy.start()

        @pl.when(has_tokens(doc))
        def _(i=i):
            for copy in copies(i):
                copy.start()

    for peer in range(peers):
        for row in range(rows):
            start = (peer * rows + row) * LANES
            at = docs * rows + row * many
            send_ref[peer, at : at + many, :] = query_ref[:, start : start + LANES]

    for i, (layer, doc) in enumerate(pairs):
        if doc == 0:
            for copy in bases(layer):
                copy.wait()

        @pl.when(has_tokens(doc))
        def _(i=i, layer=layer, doc=doc):
            for copy in copies(i):
                copy.wait()
            out_rows = lax.dot_general(
                outg_buf[i], outb[layer], BY_LAST, preferred_element_type=jnp.float32
            )
            in_rows = lax.dot_general(
                act_buf[i], inb[layer], BY_LAST, preferred_element_type=jnp.float32
            )
            position = first + lax.broadcasted_iota(jnp.int32, out_rows.shape, 0)
            out_rows = jnp.where(position < length_ref[doc], out_rows, 0.0).astype(jnp.bfloat16)
            square[...] = lax.dot_general(
                out_rows, in_rows.astype(jnp.bfloat16), BY_FIRST, preferred_element_type=jnp.float32
            )
            scale = lax.rsqrt(jnp.full((1, 1), length_ref[doc], jnp.int32).astype(jnp.float32))
            flat = scale * jnp.concatenate(
                [square[pl.ds(0, rank // 2, stride=2), :], square[pl.ds(1, rank // 2, stride=2), :]],
                axis=1,
            )
            for j in range(per_layer):
                send_ref[layer * per_layer + j, doc * rows : (doc + 1) * rows, :] = flat[
                    j * rows : (j + 1) * rows
                ]

        @pl.when(jnp.logical_not(has_tokens(doc)))
        def _(layer=layer, doc=doc):
            for j in range(per_layer):
                send_ref[layer * per_layer + j, doc * rows : (doc + 1) * rows, :] = jnp.zeros(
                    (rows, LANES), jnp.float32
                )


def score_kernel(docs, rows, many, dp, rank_ref, got_ref, send_ref):
    peers = got_ref.shape[0]
    total = dp * docs
    sums = []
    for d in range(dp):
        part = got_ref[d, : docs * rows, :]
        for c in range(1, peers // dp):
            part = part + got_ref[c * dp + d, : docs * rows, :]
        sums.append(part)
    score = jnp.zeros((total, peers * many), jnp.float32)
    for row in range(rows):
        grad = jnp.concatenate(
            [sums[d][k * rows + row : k * rows + row + 1] for d in range(dp) for k in range(docs)], axis=0
        )
        at = docs * rows + row * many
        query = got_ref[:, at : at + many, :].reshape(peers * many, LANES)
        score = score + lax.dot_general(
            grad, query, BY_LAST, precision=lax.Precision.HIGHEST, preferred_element_type=jnp.float32
        )
    placed = []
    for want in range(total):
        line = jnp.zeros((1, peers * many), jnp.float32)
        for k in range(total):
            line = jnp.where(rank_ref[k] == want, score[k : k + 1], line)
        placed.append(line)
    for d in range(dp):
        mine = jnp.concatenate(placed[d * docs : (d + 1) * docs], axis=0)
        for c in range(peers // dp):
            send_ref[c * dp + d] = mine


def local(mesh_shape, activations, out_grads, input_basis, output_basis, query_grads, doc_length, doc_rank):
    layers, docs, tok, width = activations.shape
    rank = input_basis.shape[2]
    many = query_grads.shape[0]
    dp = mesh_shape["dp"]
    peers = mesh_shape["ctx"] * dp
    rows = layers * rank * rank // LANES // peers
    pairs = layers * docs
    anywhere = pl.BlockSpec(memory_space=pl.ANY)
    vmem = pl.BlockSpec(memory_space=pltpu.VMEM)
    smem = pl.BlockSpec(memory_space=pltpu.SMEM)
    send = pl.pallas_call(
        partial_kernel,
        out_shape=jax.ShapeDtypeStruct((peers, (docs + many) * rows, LANES), jnp.float32),
        in_specs=[smem, anywhere, anywhere, anywhere, anywhere, vmem],
        out_specs=vmem,
        scratch_shapes=[
            pltpu.VMEM((pairs, tok, width), jnp.bfloat16),
            pltpu.VMEM((pairs, tok, width), jnp.bfloat16),
            pltpu.VMEM((layers, rank, width), jnp.bfloat16),
            pltpu.VMEM((layers, rank, width), jnp.bfloat16),
            pltpu.VMEM((rank, rank), jnp.float32),
            pltpu.SemaphoreType.DMA((pairs,)),
            pltpu.SemaphoreType.DMA((pairs,)),
            pltpu.SemaphoreType.DMA((layers, 2)),
        ],
        compiler_params=pltpu.CompilerParams(vmem_limit_bytes=60 << 20),
        name="partial_grads",
    )(
        doc_length,
        activations,
        out_grads,
        jnp.swapaxes(input_basis, 1, 2),
        jnp.swapaxes(output_basis, 1, 2),
        query_grads,
    )
    got = lax.all_to_all(send, ("ctx", "dp"), 0, 0)
    scores = pl.pallas_call(
        functools.partial(score_kernel, docs, rows, many, dp),
        out_shape=jax.ShapeDtypeStruct((peers, docs, peers * many), jnp.float32),
        in_specs=[smem, vmem],
        out_specs=vmem,
        compiler_params=pltpu.CompilerParams(vmem_limit_bytes=8 << 20),
        name="column_scores",
    )(doc_rank, got)
    got = lax.all_to_all(scores, ("ctx", "dp"), 0, 0)
    return jnp.sum(got, axis=0)


def solution(mesh):
    return jax.shard_map(
        functools.partial(local, dict(mesh.shape)),
        mesh=mesh,
        in_specs=(
            P(None, ("groups", "dp"), "ctx", None),
            P(None, ("groups", "dp"), "ctx", None),
            P(),
            P(),
            P(("groups", "ctx", "dp"), None),
            P(("groups", "dp")),
            P("groups"),
        ),
        out_specs=P(("groups", "dp"), None),
        check_vma=False,
    )
```

profile of v0, /device:TPU:0, one launch (start us, length us, event | category | flops | bytes accessed | tf_op | source)
XLA Modules:
  0.0 39.5 jit_solution(6067874996849230586)
XLA Ops:
  0.0 0.0 copy-start
  0.0 11.8 %partial_grads.1 = f32[16,40,128]{2,1,0:T(8,128)} custom-call(s32[2]{0:T(128)} %length_ref.1, bf16[2,2,320,4096]{3,2,1,0:T(8,128)(2,1)} %act_ref.1, bf16[2,2,320,4096]{3,2,1,0:T(8,128)(2,1)} %outg_ref.1, bf16[2,64,4096]{2,1,0:T(8,128)(2,1)} %bitcast.2, bf16[2,64,4096]{2,1,0:T(8,128)(2,1)} %bitcast.3, f32[8,8192]{1,0:T(8,128)} %query_ref.1), custom_call_target="tpu_custom_call" | custom-call | tf_op jit(solution)/shard_map/partial_grads/pallas_call | solution.py:140
  11.8 16.5 %all_to_all.10.got_ref = f32[16,40,128]{2,1,0:T(8,128)S(1)} all-to-all(f32[16,40,128]{2,1,0:T(8,128)} %partial_grads.1), channel_id=1, replica_groups=mesh['groups'=2,'ctx'=8,'dp'=2] {'ctx','dp'}, dimensions={0} | all-to-all | bytes 655360 | tf_op jit(solution)/shard_map/all_to_all | solution.py:165
  28.3 0.0 copy-done
  28.3 1.1 %column_scores.1 = f32[16,2,128]{2,1,0:T(2,128)S(1)} custom-call(s32[4]{0:T(128)S(1)} %copy-done, f32[16,40,128]{2,1,0:T(8,128)S(1)} %all_to_all.10.got_ref), custom_call_target="tpu_custom_call" | custom-call | tf_op jit(solution)/shard_map/column_scores/pallas_call | solution.py:166
  29.4 9.5 %all_to_all.11 = f32[16,2,128]{2,1,0:T(2,128)S(1)} all-to-all(f32[16,2,128]{2,1,0:T(2,128)S(1)} %column_scores.1), channel_id=1, replica_groups=mesh['groups'=2,'ctx'=8,'dp'=2] {'ctx','dp'}, dimensions={0} | all-to-all | bytes 32768 | tf_op jit(solution)/shard_map/all_to_all | solution.py:174
  38.9 0.6 %reduce_sum.9 = f32[2,128]{1,0:T(2,128)} reduce(f32[16,2,128]{2,1,0:T(2,128)S(1)} %all_to_all.11, f32[]{:T(128)} %constant.0.clone.1), dimensions={0}, to_apply=%region_0.0 | reduce | flops 3840 | bytes 17412 | tf_op jit(solution)/shard_map/reduce_sum | solution.py:175
Async XLA Ops:
  0.0 28.3 %copy-start = (s32[4]{0:T(128)S(1)}, s32[4]{0:T(128)}, u32[]{:S(2)}) copy-start(s32[4]{0:T(128)} %rank_ref.1) | copy-start | bytes 52
where the time goes:
time: 40.3 us; the launch traced here: 39.5 us
  blocking collectives  26 us (65%)
  Pallas kernels  12.9 us (32%)
  other arithmetic  0.59 us (1%)
    all_to_all x1, blocking collectives, local(): got = lax.all_to_all(send, ('ctx', 'dp'), 0, 0)  16.5 us
    pallas_call x1, Pallas kernels, local(): pl.pallas_call(partial_kernel, out_shape=jax.ShapeDtypeStruct((peers, (do...  11.8 us
    all_to_all x1, blocking collectives, local(): got = lax.all_to_all(scores, ('ctx', 'dp'), 0, 0)  9.54 us
    pallas_call x1, Pallas kernels, local(): pl.pallas_call(functools.partial(score_kernel, docs, rows, many, dp), out...  1.07 us

commit v1 on v0

--- a/solution.py
+++ b/solution.py
@@ -13,23 +13,23 @@
 
 
 def partial_kernel(
-    length_ref, act_ref, outg_ref, inb_ref, outb_ref, query_ref, send_ref,
-    act_buf, outg_buf, inb, outb, square, act_sem, outg_sem, basis_sem,
+    length_hbm, act_ref, outg_ref, inb_ref, outb_ref, query_hbm, send_ref,
+    act_buf, outg_buf, inb, outb, query, rows_out, rows_in, square, flat, length_ref, act_sem, outg_sem, basis_sem, small_sem,
 ):
     layers, docs, tok, _ = act_ref.shape
     rank = inb_ref.shape[1]
     peers = send_ref.shape[0]
     per_layer = peers // layers
     rows = rank * rank // LANES // per_layer
-    many = query_ref.shape[0]
+    many = query.shape[0]
     first = lax.axis_index("ctx") * tok
-    pairs = [(layer, doc) for layer in range(layers) for doc in range(docs)]
-
-    def copies(i):
-        layer, doc = pairs[i]
+    pairs = layers * docs
+
+    def copies(pair):
+        layer, doc = pair // docs, pair % docs
         return (
-            pltpu.make_async_copy(outg_ref.at[layer, doc], outg_buf.at[i], outg_sem.at[i]),
-            pltpu.make_async_copy(act_ref.at[layer, doc], act_buf.at[i], act_sem.at[i]),
+            pltpu.make_async_copy(outg_ref.at[layer, doc], outg_buf.at[pair], outg_sem.at[pair]),
+            pltpu.make_async_copy(act_ref.at[layer, doc], act_buf.at[pair], act_sem.at[pair]),
         )
 
     def bases(layer):
@@ -38,61 +38,85 @@
             pltpu.make_async_copy(inb_ref.at[layer], inb.at[layer], basis_sem.at[layer, 1]),
         )
 
-    def has_tokens(doc):
-        return first < length_ref[doc]
-
-    for i, (layer, doc) in enumerate(pairs):
-        if doc == 0:
-            for copy in bases(layer):
+    def valid(pair):
+        return first < length_ref[pair % docs]
+
+    lengths = pltpu.make_async_copy(length_hbm, length_ref, small_sem.at[0])
+    queries = pltpu.make_async_copy(query_hbm, query, small_sem.at[1])
+    lengths.start()
+    queries.start()
+    for copy in bases(0):
+        copy.start()
+    lengths.wait()
+    for pair in range(pairs):
+        if pair > 0 and pair % docs == 0:
+            for copy in bases(pair // docs):
                 copy.start()
 
-        @pl.when(has_tokens(doc))
-        def _(i=i):
-            for copy in copies(i):
+        @pl.when(valid(pair))
+        def _(pair=pair):
+            for copy in copies(pair):
                 copy.start()
 
+    queries.wait()
     for peer in range(peers):
         for row in range(rows):
-            start = (peer * rows + row) * LANES
+            column = (peer * rows + row) * LANES
             at = docs * rows + row * many
-            send_ref[peer, at : at + many, :] = query_ref[:, start : start + LANES]
-
-    for i, (layer, doc) in enumerate(pairs):
-        if doc == 0:
+            send_ref[peer, at : at + many, :] = query[:, column : column + LANES]
+
+    def finish(pair):
+        scale = lax.rsqrt(jnp.full((1, 1), length_ref[(pair + docs - 1) % docs], jnp.int32).astype(jnp.float32))
+        other = (pair + 1) % 2
+        square[...] = scale * lax.dot_general(
+            rows_out[other], rows_in[other], BY_FIRST, preferred_element_type=jnp.float32
+        )
+        flat[pair] = jnp.concatenate(
+            [square[pl.ds(0, rank // 2, stride=2), :], square[pl.ds(1, rank // 2, stride=2), :]], axis=1
+        )
+
+    def work(pair, _):
+        layer, doc, slot = pair // docs, pair % docs, pair % 2
+
+        @pl.when(doc == 0)
+        def _():
             for copy in bases(layer):
                 copy.wait()
 
-        @pl.when(has_tokens(doc))
-        def _(i=i, layer=layer, doc=doc):
-            for copy in copies(i):
+        @pl.when(valid(pair))
+        def _():
+            for copy in copies(pair):
                 copy.wait()
             out_rows = lax.dot_general(
-                outg_buf[i], outb[layer], BY_LAST, preferred_element_type=jnp.float32
+                outg_buf[pair], outb[layer], BY_LAST, preferred_element_type=jnp.float32
             )
             in_rows = lax.dot_general(
-                act_buf[i], inb[layer], BY_LAST, preferred_element_type=jnp.float32
+                act_buf[pair], inb[layer], BY_LAST, preferred_element_type=jnp.float32
             )
+            finish(pair)
             position = first + lax.broadcasted_iota(jnp.int32, out_rows.shape, 0)
-            out_rows = jnp.where(position < length_ref[doc], out_rows, 0.0).astype(jnp.bfloat16)
-            square[...] = lax.dot_general(
-                out_rows, in_rows.astype(jnp.bfloat16), BY_FIRST, preferred_element_type=jnp.float32
-            )
-            scale = lax.rsqrt(jnp.full((1, 1), length_ref[doc], jnp.int32).astype(jnp.float32))
-            flat = scale * jnp.concatenate(
-                [square[pl.ds(0, rank // 2, stride=2), :], square[pl.ds(1, rank // 2, stride=2), :]],
-                axis=1,
-            )
+            out_rows = jnp.where(position < length_ref[doc], out_rows, 0.0)
+            rows_out[slot] = out_rows.astype(jnp.bfloat16)
+            rows_in[slot] = in_rows.astype(jnp.bfloat16)
+
+        @pl.when(jnp.logical_not(valid(pair)))
+        def _():
+            finish(pair)
+            rows_out[slot] = jnp.zeros((tok, rank), jnp.bfloat16)
+            rows_in[slot] = jnp.zeros((tok, rank), jnp.bfloat16)
+
+        return 0
+
+    rows_out[1] = jnp.zeros((tok, rank), jnp.bfloat16)
+    rows_in[1] = jnp.zeros((tok, rank), jnp.bfloat16)
+    lax.fori_loop(0, pairs, work, 0)
+    finish(pairs)
+    for layer in range(layers):
+        for doc in range(docs):
             for j in range(per_layer):
                 send_ref[layer * per_layer + j, doc * rows : (doc + 1) * rows, :] = flat[
-                    j * rows : (j + 1) * rows
+                    layer * docs + doc + 1, j * rows : (j + 1) * rows
                 ]
-
-        @pl.when(jnp.logical_not(has_tokens(doc)))
-        def _(layer=layer, doc=doc):
-            for j in range(per_layer):
-                send_ref[layer * per_layer + j, doc * rows : (doc + 1) * rows, :] = jnp.zeros(
-                    (rows, LANES), jnp.float32
-                )
 
 
 def score_kernel(docs, rows, many, dp, rank_ref, got_ref, send_ref):
@@ -140,17 +164,23 @@
     send = pl.pallas_call(
         partial_kernel,
         out_shape=jax.ShapeDtypeStruct((peers, (docs + many) * rows, LANES), jnp.float32),
-        in_specs=[smem, anywhere, anywhere, anywhere, anywhere, vmem],
+        in_specs=[anywhere] * 6,
         out_specs=vmem,
         scratch_shapes=[
             pltpu.VMEM((pairs, tok, width), jnp.bfloat16),
             pltpu.VMEM((pairs, tok, width), jnp.bfloat16),
             pltpu.VMEM((layers, rank, width), jnp.bfloat16),
             pltpu.VMEM((layers, rank, width), jnp.bfloat16),
+            pltpu.VMEM(query_grads.shape, jnp.float32),
+            pltpu.VMEM((2, tok, rank), jnp.bfloat16),
+            pltpu.VMEM((2, tok, rank), jnp.bfloat16),
             pltpu.VMEM((rank, rank), jnp.float32),
+            pltpu.VMEM((pairs + 1, rank // 2, 2 * rank), jnp.float32),
+            pltpu.SMEM((docs,), jnp.int32),
             pltpu.SemaphoreType.DMA((pairs,)),
             pltpu.SemaphoreType.DMA((pairs,)),
             pltpu.SemaphoreType.DMA((layers, 2)),
+            pltpu.SemaphoreType.DMA((2,)),
         ],
         compiler_params=pltpu.CompilerParams(vmem_limit_bytes=60 << 20),
         name="partial_grads",

time: 40.3 us -> 39.5 us (0.980)
  Pallas kernels: 12.9 us -> 12.1 us
    pallas_call x1, Pallas kernels: 11.8 us -> 11 us  [local(): pl.pallas_call(partial_kernel, out_shape=jax.ShapeDtypeStruct((peers, (do...]
where the time goes in v1:
time: 39.5 us; the launch traced here: 38.7 us
  blocking collectives  26.1 us (66%)
  Pallas kernels  12.1 us (31%)
  other arithmetic  0.59 us (1%)
    all_to_all x1, blocking collectives, local(): got = lax.all_to_all(send, ('ctx', 'dp'), 0, 0)  16.5 us
    pallas_call x1, Pallas kernels, local(): pl.pallas_call(partial_kernel, out_shape=jax.ShapeDtypeStruct((peers, (do...  11 us
    all_to_all x1, blocking collectives, local(): got = lax.all_to_all(scores, ('ctx', 'dp'), 0, 0)  9.54 us
    pallas_call x1, Pallas kernels, local(): pl.pallas_call(functools.partial(score_kernel, docs, rows, many, dp), out...  1.07 us

profile of v1, /device:TPU:0, one launch (start us, length us, event | category | flops | bytes accessed | tf_op | source)
XLA Modules:
  0.0 38.7 jit_solution(14897515387087319417)
XLA Ops:
  0.0 0.0 copy-start
  0.0 11.0 %partial_grads.1 = f32[16,40,128]{2,1,0:T(8,128)} custom-call(s32[2]{0:T(128)} %length_hbm.1, bf16[2,2,320,4096]{3,2,1,0:T(8,128)(2,1)} %act_ref.1, bf16[2,2,320,4096]{3,2,1,0:T(8,128)(2,1)} %outg_ref.1, bf16[2,64,4096]{2,1,0:T(8,128)(2,1)} %bitcast.2, bf16[2,64,4096]{2,1,0:T(8,128)(2,1)} %bitcast.3, f32[8,8192]{1,0:T(8,128)} %query_hbm.1), custom_call_target="tpu_custom_call" | custom-call | tf_op jit(solution)/shard_map/partial_grads/pallas_call | solution.py:164
  11.0 16.5 %all_to_all.10.got_ref = f32[16,40,128]{2,1,0:T(8,128)S(1)} all-to-all(f32[16,40,128]{2,1,0:T(8,128)} %partial_grads.1), channel_id=1, replica_groups=mesh['groups'=2,'ctx'=8,'dp'=2] {'ctx','dp'}, dimensions={0} | all-to-all | bytes 655360 | tf_op jit(solution)/shard_map/all_to_all | solution.py:195
  27.5 0.0 copy-done
  27.5 1.1 %column_scores.1 = f32[16,2,128]{2,1,0:T(2,128)S(1)} custom-call(s32[4]{0:T(128)S(1)} %copy-done, f32[16,40,128]{2,1,0:T(8,128)S(1)} %all_to_all.10.got_ref), custom_call_target="tpu_custom_call" | custom-call | tf_op jit(solution)/shard_map/column_scores/pallas_call | solution.py:196
  28.6 9.5 %all_to_all.11 = f32[16,2,128]{2,1,0:T(2,128)S(1)} all-to-all(f32[16,2,128]{2,1,0:T(2,128)S(1)} %column_scores.1), channel_id=1, replica_groups=mesh['groups'=2,'ctx'=8,'dp'=2] {'ctx','dp'}, dimensions={0} | all-to-all | bytes 32768 | tf_op jit(solution)/shard_map/all_to_all | solution.py:204
  38.2 0.6 %reduce_sum.9 = f32[2,128]{1,0:T(2,128)} reduce(f32[16,2,128]{2,1,0:T(2,128)S(1)} %all_to_all.11, f32[]{:T(128)} %constant.0.clone.1), dimensions={0}, to_apply=%region_0.0 | reduce | flops 3840 | bytes 17412 | tf_op jit(solution)/shard_map/reduce_sum | solution.py:205
Async XLA Ops:
  0.0 27.5 %copy-start = (s32[4]{0:T(128)S(1)}, s32[4]{0:T(128)}, u32[]{:S(2)}) copy-start(s32[4]{0:T(128)} %rank_ref.1) | copy-start | bytes 52
